TPU v7x, 512 devices: a whole 4x8x8 slice. The times are simulated.
512 devices in a mesh: group: 64 (over z_hi, y, core), tp: 8 (over z_lo, x).
Axes of the slice: x: 4, y: 8, z: 8 (z_hi: 4, z_lo: 2; z = z_hi * 2 + z_lo), core: 2. Of those that a mesh axis runs over, the one named last changes fastest.
Arguments:
- hidden: bfloat16 [2, 4096, 8192], P(None, 'group', 'tp'), may hold values from -6 to 6
- queries: bfloat16 [2, 4096, 8, 512], P(None, 'group', 'tp'), may hold values from -16 to 16
- kv_cache: bfloat16 [4096, 8, 64, 256], P('group', 'tp'), may hold values from -16 to 16
- lengths: int32 [4096], P('group'), may hold values from 2 to 128, as said below
- weights: bfloat16 [64, 8192, 1024], P('group', None, 'tp'), may hold values from -0.0625 to 0.0625
- kv_bias: bfloat16 [64, 1024], P('group', 'tp'), may hold values from -3 to 3
- owner_group: int32 [1], replicated, may hold values from 0 to 63
Outputs:
- attended: bfloat16 [2, 4096, 4096], P(None, 'group', 'tp')
Inputs may be any that keep to these rules, and one draw needn't show every extreme that they name: `lengths`: some row holds exactly 128 cached tokens.
All inputs are finite; a program needn't handle non-finite values.
Results may differ from a plain program's by a relative error of at most 0.0043.
Values may be sent and summed in bfloat16 or wider, within the bound.
A program may use at most 64 MiB of HBM per device.

v0:
```python
import math

import jax
import jax.numpy as jnp
from jax import lax
from jax.sharding import PartitionSpec as P

KVH = 4


def shifted(x, axis, by):
    peers = lax.axis_size(axis)
    pairs = [(i, i + by) for i in range(peers) if 0 <= i + by < peers]
    return lax.ppermute(x, axis, pairs)


def spread(value, axis, source):
    kept = jnp.where(lax.axis_index(axis) == source, value, 0).astype(value.dtype)
    return lax.psum(kept, axis)


def from_partner(x, axis, distance):
    return lax.ppermute(x, axis, [(i, i ^ 1 << distance) for i in range(lax.axis_size(axis))])


def rotate(key_part, positions):
    head_width = key_part.shape[-1]
    half_width = head_width // 2
    freq = jnp.exp(
        -(jnp.arange(half_width, dtype=jnp.float32) * (2.0 / head_width)) * math.log(1000000.0)
    )
    angle = positions[:, None, None] * freq[None, None, :]
    cosine = jnp.cos(angle)
    sine = jnp.sin(angle)
    first_half = key_part[..., :half_width]
    second_half = key_part[..., half_width:]
    return jnp.concatenate(
        [first_half * cosine - second_half * sine, second_half * cosine + first_half * sine], -1
    )


def merge_splits(first_split, second_split):
    peak_score = jnp.maximum(first_split[1], second_split[1])
    first_scale = jnp.exp(first_split[1] - peak_score)
    second_scale = jnp.exp(second_split[1] - peak_score)
    top_part = first_split[0] * first_scale[..., None] + second_split[0] * second_scale[..., None]
    bottom_part = first_split[2] * first_scale + second_split[2] * second_scale
    return top_part / bottom_part[..., None]


def split_partials(
    query_heads, cache_part, half_index, row_lengths, new_keys, new_values, take_new
):
    head_width = query_heads.shape[-1]
    score_scale = 1.0 / math.sqrt(head_width)
    half_len = cache_part.shape[2]
    key_part = cache_part[..., :head_width]
    value_part = cache_part[..., head_width:]
    scores = (
        jnp.einsum("rsqd,rscd->rsqc", query_heads, key_part, preferred_element_type=jnp.float32)
        * score_scale
    )
    new_scores = (
        jnp.einsum("rsqd,rsnd->rsqn", query_heads, new_keys, preferred_element_type=jnp.float32)
        * score_scale
    )
    pos_ids = half_index[:, None] * half_len + jnp.arange(half_len, dtype=jnp.int32)[None, :]
    usable = (pos_ids[None, :, :] < row_lengths[:, None, None])[:, :, None, :]
    usable_new = take_new[None, :, None, None]
    peak_score = jnp.maximum(
        jnp.max(jnp.where(usable, scores, -1e30), -1),
        jnp.max(jnp.where(usable_new, new_scores, -1e30), -1),
    )
    cache_weights = jnp.where(usable, jnp.exp(scores - peak_score[..., None]), 0.0)
    new_weights = jnp.where(usable_new, jnp.exp(new_scores - peak_score[..., None]), 0.0)
    summed = jnp.sum(cache_weights, -1) + jnp.sum(new_weights, -1)
    weighted = jnp.einsum(
        "rsqc,rscd->rsqd",
        cache_weights.astype(jnp.bfloat16),
        value_part,
        preferred_element_type=jnp.float32,
    )
    weighted = weighted + jnp.einsum(
        "rsqn,rsnd->rsqd",
        new_weights.astype(jnp.bfloat16),
        new_values,
        preferred_element_type=jnp.float32,
    )
    return (weighted, peak_score, summed)


def on_device(hidden, queries, kv_cache, lengths, weights, kv_bias, owner_group):
    slot_count = queries.shape[2]
    head_width = kv_cache.shape[3] // 2
    row_count = queries.shape[1]
    top_bit = lax.axis_size("tp").bit_length() - 2
    upper_reach = -(lax.axis_size("tp") // 2)
    slot_kind = (lax.axis_index("tp") * slot_count + jnp.arange(slot_count, dtype=jnp.int32)) // KVH
    is_first = slot_kind == 0
    positions = lengths.astype(jnp.float32)

    def fold_rows(panel_rows, matrix):
        return jnp.dot(
            lax.all_gather(panel_rows, "tp", axis=1, tiled=True),
            matrix,
            preferred_element_type=jnp.float32,
        )

    def new_entries(running, bias_row, offset_pos):
        summed = (running + bias_row.astype(jnp.float32)[None, :]).reshape(
            row_count, slot_count, head_width
        )
        summed = jnp.where(
            is_first[None, :, None], rotate(summed, positions + offset_pos), summed
        ).astype(jnp.bfloat16)
        partner = shifted(summed, "tp", upper_reach)
        new_key = jnp.where(is_first[None, :, None], summed, partner)
        new_value = jnp.where(is_first[None, :, None], partner, summed)
        return (new_key, new_value)

    fresh_weights, fresh_bias = (
        spread(weights, "group", owner_group[0]),
        spread(kv_bias, "group", owner_group[0]),
    )
    first_sum = fold_rows(hidden[0], weights[0])
    second_sum = fold_rows(hidden[1], fresh_weights[0])
    key_first, value_first = new_entries(first_sum, kv_bias[0], 0.0)
    key_second, value_second = new_entries(second_sum, fresh_bias[0], 1.0)

    def attend(step_index, new_keys, new_values):
        own_queries = queries[step_index]
        other_queries = from_partner(own_queries, "tp", top_bit)
        all_heads = jnp.where(
            is_first[None, :, None],
            jnp.concatenate([own_queries, other_queries], -1),
            jnp.concatenate([other_queries, own_queries], -1),
        )
        all_heads = all_heads.reshape(row_count, slot_count, 8, head_width)
        weighted, peak_score, summed = split_partials(
            all_heads, kv_cache, slot_kind, lengths, new_keys, new_values, is_first
        )
        weighted = weighted.reshape(row_count, slot_count, 2, 4, head_width)
        peak_score = peak_score.reshape(row_count, slot_count, 2, 4)
        summed = summed.reshape(row_count, slot_count, 2, 4)
        mine_flag = is_first[None, :, None]
        mine = (
            jnp.where(mine_flag[..., None], weighted[:, :, 0], weighted[:, :, 1]),
            jnp.where(mine_flag, peak_score[:, :, 0], peak_score[:, :, 1]),
            jnp.where(mine_flag, summed[:, :, 0], summed[:, :, 1]),
        )
        outgoing = (
            jnp.where(mine_flag[..., None], weighted[:, :, 1], weighted[:, :, 0]),
            jnp.where(mine_flag, peak_score[:, :, 1], peak_score[:, :, 0]),
            jnp.where(mine_flag, summed[:, :, 1], summed[:, :, 0]),
        )
        incoming = from_partner((outgoing[0], outgoing[1], outgoing[2]), "tp", top_bit)
        merged = merge_splits(mine, incoming)
        return merged.reshape(row_count, -1).astype(jnp.bfloat16)

    first_out = attend(0, key_first[:, :, None], value_first[:, :, None])
    second_out = attend(
        1, jnp.stack([key_first, key_second], 2), jnp.stack([value_first, value_second], 2)
    )
    return jnp.stack([first_out, second_out])


def solution(mesh):
    in_specs = (
        P(None, "group", "tp"),
        P(None, "group", "tp", None),
        P("group", "tp", None, None),
        P("group"),
        P("group", None, "tp"),
        P("group", "tp"),
        P(),
    )
    out_specs = P(None, "group", "tp")
    return jax.shard_map(
        on_device, mesh=mesh, in_specs=in_specs, out_specs=out_specs, check_vma=False
    )
```

profile of v0, /device:TPU:1, one launch (start us, length us, event | category | flops | bytes accessed | tf_op | source)
XLA Modules:
  0.0 618.1 jit_solution(3344665842218165569)
XLA Ops:
  7.4 0.0 all-gather.5.cloned.1.call-start
  7.4 1.7 fusion.81
  9.0 0.0 all-gather.5.cloned.1.call-update
  9.1 0.0 all-gather.7.cloned.1.call-start
  9.1 0.7 all-gather.7.cloned.1.call-update
  9.8 0.0 all-reduce.2.cloned.1.call-start
  10.5 1.5 select_bitcast_fusion
  12.0 0.0 all-reduce.2.cloned.1.call-update
  12.0 0.9 copy-done.2
  12.9 4.8 collective-permute-start
  17.8 1.9 collective-permute-start.5
  19.7 0.0 copy-done.3
  19.7 0.1 broadcast_compare_fusion
  19.8 0.0 copy-done.4
  19.9 145.1 %psum.15 = bf16[128]{0:T(256)(128)(2,1)S(1)} all-reduce(bf16[128]{0:T(256)(128)(2,1)S(1)} %get-tuple-element.35), channel_id=1, replica_groups=mesh['group'=64,'tp'=8] {'group'}, use_global_device_ids=true, to_apply=%region_4.5 | all-reduce | flops 128 | bytes 512 | tf_op jit(solution)/shard_map/psum | solution.py:19
  165.0 0.0 collective-permute-done
  165.1 0.0 collective-permute-done.5
  165.1 2.0 select_reduce_fusion.1
  167.1 0.0 copy-done
  167.1 1.7 fusion.2
  168.8 0.0 copy-start.1
  168.8 0.0 all-gather.7.cloned.1.call-done
  168.8 411.0 %all-reduce.2.cloned.1.call-done = bf16[8192,128]{1,0:T(8,128)(2,1)} async-done(((bf16[8192,128]{1,0:T(8,128)(2,1)}), bf16[8192,128]{1,0:T(8,128)(2,1)}) %all-reduce.2.cloned.1.call-update) | async-done | bytes 2097168 | tf_op jit(solution)/shard_map/psum | solution.py:19
  579.8 2.4 convolution_add_fusion.1
  582.2 0.3 fusion.40
  582.6 0.1 fusion.55
  582.6 1.3 collective-permute-start.1
  583.9 0.1 fusion.54
  584.0 1.3 collective-permute-start.6
  585.3 1.8 collective-permute-done.1
  587.1 0.2 fusion.52
  587.4 0.1 copy.50
  587.5 1.0 collective-permute-done.6
  588.5 0.7 fusion.9
  589.3 0.3 select_reduce_fusion.2
  589.5 0.1 copy.61
  589.6 0.2 fusion.11
  589.8 0.4 fusion.7
  590.3 1.9 collective-permute-start.2
  592.2 0.1 copy.55
  592.3 3.4 collective-permute-start.4
  595.7 0.5 multiply_add_fusion
  596.2 1.9 collective-permute-start.3
  598.1 0.1 fusion.60
  598.3 0.1 copy.64
  598.3 3.4 collective-permute-start.9
  601.7 1.9 collective-permute-start.7
  603.6 0.3 convolution_add_fusion
  604.0 0.0 collective-permute-done.2
  604.0 3.4 collective-permute-start.8
  607.4 0.0 collective-permute-done.4
  607.4 0.0 collective-permute-done.7
  607.4 0.1 copy.54
  607.5 0.1 copy.56
  607.6 0.1 copy.51
  607.7 0.0 collective-permute-done.9
  607.7 0.1 copy.63
  607.8 0.1 copy.65
  607.9 0.1 copy.62
  608.0 0.0 collective-permute-done.3
  608.0 0.3 fusion.30
  608.3 1.4 collective-permute-done.8
  609.7 0.3 fusion.29
  610.0 0.7 pad_maximum_fusion
  (36 shorter events, 0.4 us)
Async XLA Ops:
  7.4 159.7 %all-gather.5.cloned.1.call-start = ((), (), s32[]{:S(2)}) async-start(), calls=%async_computation.1 | async-start | bytes 1179648 | tf_op jit(solution)/shard_map/all_gather | solution.py:104
  9.1 159.8 %all-gather.7.cloned.1.call-start = ((), (), s32[]{:S(2)}) async-start(), calls=%async_computation.2 | async-start | bytes 1179648 | tf_op jit(solution)/shard_map/all_gather | solution.py:104
  9.8 570.0 %all-reduce.2.cloned.1.call-start = ((), (), s32[]{:S(2)}) async-start(), calls=%async_computation | async-start | bytes 4194304 | tf_op jit(solution)/shard_map/psum | solution.py:19
  12.0 0.9 copy-start.2
  12.0 7.7 %copy-start.3 = (s32[64]{0:T(128)S(1)}, s32[64]{0:T(128)}, u32[]{:S(2)}) copy-start(s32[64]{0:T(128)} %param.10) | copy-start | bytes 772
  12.0 7.8 %copy-start.4 = (bf16[1,128]{1,0:T(2,128)(2,1)S(1)}, bf16[1,128]{1,0:T(2,128)(2,1)}, u32[]{:S(2)}) copy-start(bf16[1,128]{1,0:T(2,128)(2,1)} %param.12) | copy-start | bytes 772
  12.0 155.1 %copy-start = (bf16[1,8192,128]{2,1,0:T(8,128)(2,1)S(1)}, bf16[1,8192,128]{2,1,0:T(8,128)(2,1)}, u32[]{:S(2)}) copy-start(bf16[1,8192,128]{2,1,0:T(8,128)(2,1)} %param.11) | copy-start | bytes 6291460
  12.9 152.1 %collective-permute-start = (bf16[64,1,512]{2,0,1:T(8,128)(2,1)S(1)}, bf16[64,1,512]{2,0,1:T(8,128)(2,1)S(1)}, u32[]{:S(2)}, u32[]{:S(2)}) collective-permute-start(bf16[64,1,512]{2,0,1:T(8,128)(2,1)S(1)} %get-tuple-element.14), channel_id=1, source_target_pairs={{0,4},{1,5},{2,6},{3,7},{4,0},{5,1},{6,2},{7,3},{8,12},{9,13},{10,... | collective-permute-start | bytes 196616 | tf_op jit(solution)/shard_map/ppermute | solution.py:23
  17.8 147.3 %collective-permute-start.5 = (bf16[64,1,512]{2,0,1:T(8,128)(2,1)S(1)}, bf16[64,1,512]{2,0,1:T(8,128)(2,1)S(1)}, u32[]{:S(2)}, u32[]{:S(2)}) collective-permute-start(bf16[64,1,512]{2,0,1:T(8,128)(2,1)S(1)} %get-tuple-element.15), channel_id=1, source_target_pairs={{0,4},{1,5},{2,6},{3,7},{4,0},{5,1},{6,2},{7,3},{8,12},{9,13},{10,... | collective-permute-start | bytes 196616 | tf_op jit(solution)/shard_map/ppermute | solution.py:23
  168.8 419.7 %copy-start.1 = (bf16[64,1,64,256]{3,2,1,0:T(8,128)(2,1)S(1)}, bf16[64,1,64,256]{3,2,1,0:T(8,128)(2,1)}, u32[]{:S(2)}) copy-start(bf16[64,1,64,256]{3,2,1,0:T(8,128)(2,1)} %param.9) | copy-start | bytes 6291460
  582.6 4.5 collective-permute-start.1
  584.0 4.5 collective-permute-start.6
  590.3 13.7 %collective-permute-start.2 = (f32[64,1,4]{0,2,1:T(4,128)S(1)}, f32[64,1,4]{0,2,1:T(4,128)S(1)}, u32[]{:S(2)}, u32[]{:S(2)}) collective-permute-start(f32[64,1,4]{0,2,1:T(4,128)S(1)} %select_bitcast_fusion.8), channel_id=1, source_target_pairs={{0,4},{1,5},{2,6},{3,7},{4,0},{5,1},{6,2},{7,3},{8,12},{9,13},{10,... | collective-permute-start | bytes 3080 | tf_op jit(solution)/shard_map/ppermute | solution.py:23
  592.3 15.1 %collective-permute-start.4 = (f32[64,1,4]{0,2,1:T(4,128)S(1)}, f32[64,1,4]{0,2,1:T(4,128)S(1)}, u32[]{:S(2)}, u32[]{:S(2)}) collective-permute-start(f32[64,1,4]{0,2,1:T(4,128)S(1)} %select_bitcast_fusion.7), channel_id=1, source_target_pairs={{0,4},{1,5},{2,6},{3,7},{4,0},{5,1},{6,2},{7,3},{8,12},{9,13},{10,... | collective-permute-start | bytes 3080 | tf_op jit(solution)/shard_map/ppermute | solution.py:23
  596.2 11.8 %collective-permute-start.3 = (f32[64,1,4,128]{3,2,0,1:T(4,128)S(1)}, f32[64,1,4,128]{3,2,0,1:T(4,128)S(1)}, u32[]{:S(2)}, u32[]{:S(2)}) collective-permute-start(f32[64,1,4,128]{3,2,0,1:T(4,128)S(1)} %select_bitcast_fusion.2), channel_id=1, source_target_pairs={{0,4},{1,5},{2,6},{3,7},{4,0},{5,1},{6,2},{7,3},{8,12},{9,13},{10,... | collective-permute-start | bytes 393224 | tf_op jit(solution)/shard_map/ppermute | solution.py:23
  598.3 9.4 %collective-permute-start.9 = (f32[64,1,4]{0,2,1:T(4,128)S(1)}, f32[64,1,4]{0,2,1:T(4,128)S(1)}, u32[]{:S(2)}, u32[]{:S(2)}) collective-permute-start(f32[64,1,4]{0,2,1:T(4,128)S(1)} %select_bitcast_fusion.5), channel_id=1, source_target_pairs={{0,4},{1,5},{2,6},{3,7},{4,0},{5,1},{6,2},{7,3},{8,12},{9,13},{10,... | collective-permute-start | bytes 3080 | tf_op jit(solution)/shard_map/ppermute | solution.py:23
  601.7 5.7 collective-permute-start.7
  604.0 5.7 collective-permute-start.8
Sparse Core Ops, SparseCore 0:
  10.3 45.7 all-gather.4
  58.4 43.2 all-gather.6
Sparse Core Ops, SparseCore 1:
  13.2 566.6 all-reduce.1
where the time goes:
time: 621 us; the launch traced here: 618 us
  waiting for transfers between devices  416 us (67%)
  blocking collectives  145 us (23%)
  starting transfers between devices  25.2 us (4%)
  between operations  15.9 us (3%)
  matrix products  8.51 us (1%)
    psum x1, waiting for transfers between devices, spread(): return lax.psum(kept, axis)  411 us
    psum x1, blocking collectives, spread(): return lax.psum(kept, axis)  145 us
    ppermute x8, starting transfers between devices, from_partner(): lax.ppermute(x, axis, [(i, i ^ 1 << distance) for i in range(lax.axis_siz...  22.6 us
  transfers between devices with their start and end apart: 13, of which 4 were waited for; matrix products, arithmetic and copies ran while one was open for 1% of the time, Pallas kernels for 0%

commit v1 on v0

v1 whole, which is shorter than its diff:
```python
import functools
import math

import jax
import jax.numpy as jnp
from jax import lax
from jax.experimental import pallas as pl
from jax.experimental.pallas import tpu as pltpu
from jax.sharding import PartitionSpec as P

MESH = pl.DeviceIdType.MESH
BF16 = jnp.bfloat16
F32 = jnp.float32
NEG = -1e30
NY, NZ, NX = 8, 4, 4
LONG, SHORT = 4, 3
ROWS, D, HD, HALF, CHUNK, QUART = 64, 8192, 128, 4096, 512, 128
SCALE2 = math.log2(math.e) / math.sqrt(128.0)


def remote(src, dst, send_sem, recv_sem, device):
    return pltpu.make_async_remote_copy(
        src_ref=src, dst_ref=dst, send_sem=send_sem, recv_sem=recv_sem,
        device_id=device, device_id_type=MESH,
    )


def dot_t(a, b):
    return lax.dot_general(a, b, (((1,), (1,)), ((), ())), preferred_element_type=F32)


def kernel(
    w_hbm, kv_hbm, hid_hbm, q_hbm, len_ref, bias_ref, owner_ref, out_ref,
    wv, xbuf, rl, rs, zr, wf, hf, kvv, qo, qp,
    oo, mo, lo, po, pml, ro, rml, lenc, cosf, sinf,
    bias_mine, bias_die, bias_chip, bias_y, bias_row, bias_z,
    kvown, kvpeer, acc,
    loc_sem, die_s, die_r, rl_s, rl_r, rs_s, rs_r, z_s, z_r, zg_s, zg_r,
    al_s, al_r, as_s, as_r, df_s, df_r,
    hz_s, hz_r, hx_s, hx_r, q_s, q_r, p_s, p_r, e_s, e_r,
    bd_s, bd_r, by_s, by_r, bz_s, bz_r,
):
    group = lax.axis_index("group")
    tp = lax.axis_index("tp")
    core = group % 2
    y = (group // 2) % NY
    zh = group // (2 * NY)
    x = tp % NX
    zl = tp // NX
    step_l = 1 - 2 * core

    def at(zz, yy, cc):
        return (zz * (2 * NY) + yy * 2 + cc, tp)

    def wrap_y(v):
        return (v + 4 * NY) % NY

    sibling = at(zh, y, 1 - core)
    ahead = at(zh, wrap_y(y + step_l), core)
    behind = at(zh, wrap_y(y - step_l), core)
    z_peers = [at((zh + j) % NZ, y, core) for j in range(1, NZ)]
    y_peers = [at(zh, (y + j) % NY, core) for j in range(1, NY)]
    partner_tp = (tp + NX) % (2 * NX)
    partner = (group, partner_tp)
    x_peers = [(group, zl * NX + (x + j) % NX) for j in range(1, NX)]

    kv_copy = pltpu.make_async_copy(kv_hbm, kvv, loc_sem.at[0])
    w_copy = pltpu.make_async_copy(w_hbm, wv, loc_sem.at[1])
    h_copy = pltpu.make_async_copy(hid_hbm, hf.at[:, tp], loc_sem.at[2])
    q_copy = pltpu.make_async_copy(q_hbm, qo, loc_sem.at[3])
    w_copy.start()
    q_copy.start()
    h_copy.start()
    kv_copy.start()

    barrier = pltpu.get_barrier_semaphore()
    everyone = [sibling, partner] + x_peers + z_peers + y_peers
    for other in everyone:
        pl.semaphore_signal(barrier, inc=1, device_id=other, device_id_type=MESH)
    pl.semaphore_wait(barrier, len(everyone))

    order = []
    for s in range(LONG):
        order.append(wrap_y(y + step_l * (LONG - s)))
        if s < SHORT:
            order.append(wrap_y(y - step_l * (SHORT - s)))
    order.append(y)

    def rows_of(chunk, quarter=None):
        if quarter is None:
            return pl.ds(pl.multiple_of(chunk * CHUNK, CHUNK), CHUNK)
        return pl.ds(pl.multiple_of(chunk * CHUNK + quarter * QUART, QUART), QUART)

    def half_rows(half, chunk, quarter=None):
        if quarter is None:
            return pl.ds(pl.multiple_of(half * HALF + chunk * CHUNK, CHUNK), CHUNK)
        return pl.ds(pl.multiple_of(half * HALF + chunk * CHUNK + quarter * QUART, QUART), QUART)

    die = []
    for n in range(NY):
        if n == NY - 1:
            chunk = y
        elif n % 2 == 0:
            chunk = wrap_y(y - step_l * (LONG - n // 2))
        else:
            chunk = wrap_y(y + step_l * (SHORT - n // 2))
        die.append(remote(
            w_hbm.at[half_rows(1 - core, chunk)], xbuf.at[rows_of(chunk)],
            die_s.at[n], die_r.at[n], sibling))
        die[-1].start()

    q_send = remote(q_hbm, qp, q_s, q_r, partner)
    q_send.start()
    hz, hx = {}, {}
    for s in (1, 0):
        hz[s] = remote(hid_hbm.at[s], hf.at[s, tp], hz_s.at[s], hz_r.at[s], partner)
        hz[s].start()
        for j in range(NX - 1):
            hx[s, 0, j] = remote(
                hid_hbm.at[s], hf.at[s, tp], hx_s.at[s, 0, j], hx_r.at[s, 0, j], x_peers[j])
            hx[s, 0, j].start()

    owner = owner_ref[0]
    mine_w = jnp.full((1, HD), (owner == group).astype(F32)).astype(BF16)
    sib_w = jnp.full((1, HD), (owner == group + 1 - 2 * core).astype(F32)).astype(BF16)

    bias_mine[...] = jnp.broadcast_to(bias_ref[...] * mine_w, (16, HD))
    b_die = remote(bias_mine, bias_die, bd_s, bd_r, sibling)
    b_die.start()

    w_copy.wait()

    def combine(n):
        chunk = order[n]
        die[n].wait_recv()
        at_rows = rows_of(chunk)
        xbuf[at_rows] = wv[half_rows(core, chunk)] * mine_w + xbuf[at_rows] * sib_w

    long_send, short_send = {}, {}

    def reduce_step(s):
        chunk = wrap_y(y + step_l * (LONG - s))
        for q in range(4):
            part = pl.ds(q * QUART, QUART)
            if s == 0:
                src = xbuf.at[rows_of(chunk, q)]
            else:
                long_send[s - 1, q].wait_recv()
                rl[s - 1, part] = rl[s - 1, part] + xbuf[rows_of(chunk, q)]
                src = rl.at[s - 1, part]
            long_send[s, q] = remote(src, rl.at[s, part], rl_s.at[s, q], rl_r.at[s, q], ahead)
            long_send[s, q].start()
            if s < SHORT:
                other = wrap_y(y - step_l * (SHORT - s))
                if s == 0:
                    src = xbuf.at[rows_of(other, q)]
                else:
                    short_send[s - 1, q].wait_recv()
                    rs[s - 1, part] = rs[s - 1, part] + xbuf[rows_of(other, q)]
                    src = rs.at[s - 1, part]
                short_send[s, q] = remote(
                    src, rs.at[s, part], rs_s.at[s, q], rs_r.at[s, q], behind)
                short_send[s, q].start()

    combine(0)
    combine(1)
    reduce_step(0)
    for n in range(2, NY):
        combine(n)

    lens = jnp.broadcast_to(len_ref[...].astype(F32), (ROWS, ROWS))
    diag = lax.broadcasted_iota(jnp.int32, (ROWS, ROWS), 0) == lax.broadcasted_iota(
        jnp.int32, (ROWS, ROWS), 1)
    len_col = jnp.sum(jnp.where(diag, lens, 0.0), axis=1, keepdims=True)
    lenc[...] = jnp.broadcast_to(len_col, (ROWS, HD))

    def attend(block):
        kept = []
        for sub in range(2):
            r0 = block * 16 + sub * 8
            pieces = []
            for src in (qo, qp):
                for s in range(2):
                    for j in range(4):
                        part = src[s, pl.ds(block * 16, 16), pl.ds(j * HD, HD)].astype(F32)
                        pieces.append(part[sub * 8:sub * 8 + 8])
            lhs = jnp.concatenate(pieces, axis=0).astype(BF16)
            cache = pl.ds(r0 * 64, 512)
            scores = dot_t(lhs, kvv[cache, pl.ds(0, HD)]).reshape(16, 8, 512)
            row_id = lax.broadcasted_iota(jnp.int32, (8, 512), 0)
            col_id = lax.broadcasted_iota(jnp.int32, (8, 512), 1)
            length = lenc[pl.ds(r0, 8), :][:, :1]
            pos = (col_id % 64 + zl * 64).astype(F32)
            usable = jnp.logical_and(col_id // 64 == row_id, pos < length)[None]
            peak = jnp.max(jnp.where(usable, scores, NEG), axis=2, keepdims=True)
            weight = jnp.exp2(jnp.where(usable, (scores - peak) * SCALE2, NEG))
            total = jnp.sum(weight, axis=2, keepdims=True)
            weighted = jnp.dot(
                weight.astype(BF16).reshape(128, 512), kvv[cache, pl.ds(HD, HD)],
                preferred_element_type=F32).reshape(16, 8, HD)
            rows = pl.ds(r0, 8)
            oo[:, rows] = weighted[:8]
            mo[:, rows] = jnp.broadcast_to(peak[:8], (8, 8, HD))
            lo[:, rows] = jnp.broadcast_to(total[:8], (8, 8, HD))
            kept.append(weighted[8:])
            lane = lax.broadcasted_iota(jnp.int32, (8, HD), 1)
            packed = jnp.zeros((8, HD), F32)
            for i in range(8):
                packed = jnp.where(lane == i, peak[8 + i], packed)
                packed = jnp.where(lane == 8 + i, total[8 + i], packed)
            pml[rows] = packed
        po[:, pl.ds(block * 16, 16)] = jnp.concatenate(kept, axis=1).astype(BF16)

    q_copy.wait()
    kv_copy.wait()
    b_die.wait_recv()
    bias_chip[...] = bias_mine[...] + bias_die[...]
    b_y = [remote(bias_chip, bias_y.at[j], by_s.at[j], by_r.at[j], y_peers[j]) for j in range(NY - 1)]
    for copy in b_y:
        copy.start()
    q_send.wait_recv()
    attend(0)

    reduce_step(1)

    for s in (1, 0):
        hz[s].wait_recv()
        for j in range(NX - 1):
            hx[s, 1, j] = remote(
                hf.at[s, partner_tp], hf.at[s, partner_tp], hx_s.at[s, 1, j], hx_r.at[s, 1, j],
                x_peers[j])
            hx[s, 1, j].start()
    attend(1)

    reduce_step(2)
    attend(2)
    for copy in b_y:
        copy.wait_recv()
    total_bias = bias_chip[...]
    for j in range(NY - 1):
        total_bias = total_bias + bias_y[j]
    bias_row[...] = total_bias
    b_z = [remote(bias_row, bias_z.at[j], bz_s.at[j], bz_r.at[j], z_peers[j]) for j in range(NZ - 1)]
    for copy in b_z:
        copy.start()

    reduce_step(3)
    attend(3)
    p_send = [
        remote(po, ro, p_s.at[0], p_r.at[0], partner),
        remote(pml, rml, p_s.at[1], p_r.at[1], partner),
    ]
    for copy in p_send:
        copy.start()

    for q in range(4):
        part = pl.ds(q * QUART, QUART)
        long_send[LONG - 1, q].wait_recv()
        short_send[SHORT - 1, q].wait_recv()
        rl[LONG - 1, part] = rl[LONG - 1, part] + rs[SHORT - 1, part] + xbuf[rows_of(y, q)]
    z_send = []
    for j in range(NZ - 1):
        part = pl.ds(pl.multiple_of((zh + j + 1) % NZ * QUART, QUART), QUART)
        z_send.append(remote(rl.at[LONG - 1, part], zr.at[j], z_s.at[j], z_r.at[j], z_peers[j]))
        z_send[-1].start()

    lane = lax.broadcasted_iota(jnp.int32, (ROWS, HD), 1)
    freq = jnp.exp(-((lane % 64).astype(F32) * (2.0 / HD)) * math.log(1000000.0))
    is_key = tp < NX
    for s in range(2):
        angle = (lenc[...] + float(s)) * freq
        sine = jnp.sin(angle)
        cosf[s] = jnp.where(is_key, jnp.cos(angle), 1.0)
        sinf[s] = jnp.where(is_key, jnp.where(lane < 64, -sine, sine), 0.0)

    own_part = pl.ds(pl.multiple_of(zh * QUART, QUART), QUART)
    total_w = rl[LONG - 1, own_part]
    for j in range(NZ - 1):
        z_send[j].wait_recv()
        total_w = total_w + zr[j]
    own_rows = half_rows(core, y, zh)
    wf[own_rows] = total_w
    zg = []
    for j in range(NZ - 1):
        zg.append(remote(wf.at[own_rows], wf.at[own_rows], zg_s.at[j], zg_r.at[j], z_peers[j]))
        zg[-1].start()

    al, ash, df = {}, {}, {}

    def forward(kind, s, i, chunk):
        rows = half_rows(core, chunk, (zh - i + NZ) % NZ)
        ref = wf.at[rows]
        if kind in ("own", "long") and s < LONG:
            al[s, i] = remote(ref, ref, al_s.at[s, i], al_r.at[s, i], ahead)
            al[s, i].start()
        if kind in ("own", "short") and s < SHORT:
            ash[s, i] = remote(ref, ref, as_s.at[s, i], as_r.at[s, i], behind)
            ash[s, i].start()
        n = 0 if kind == "own" else (s if kind == "long" else LONG + s)
        df[n, i] = remote(ref, ref, df_s.at[n, i], df_r.at[n, i], sibling)
        df[n, i].start()

    forward("own", 0, 0, y)
    for i in range(1, 4):
        zg[i - 1].wait_recv()
        forward("own", 0, i, y)

    def multiply(step, weights, half, chunk):
        block = half * NY + chunk
        feats = hf[step, block // 2, :, pl.ds(pl.multiple_of((block % 2) * CHUNK, CHUNK), CHUNK)]
        return jnp.dot(feats, weights[half_rows(half, chunk)], preferred_element_type=F32)

    def wait_features(s):
        for kind in range(2):
            for j in range(NX - 1):
                hx[s, kind, j].wait_recv()

    def from_sibling(n, chunk):
        for i in range(4):
            df[n, i].wait_recv()
        acc[...] += multiply(1, wf, 1 - core, chunk)

    def entry(s, total, bias):
        total = total + bias
        turned = total * cosf[s] + pltpu.roll(total, 64, 1) * sinf[s]
        kvown[s] = turned.astype(BF16)
        send = remote(kvown.at[s], kvpeer.at[s], e_s.at[s], e_r.at[s], partner)
        send.start()
        return send

    def add_entry(s, i, query, key, value):
        score = jnp.sum(query * key, axis=1, keepdims=True)
        old = mo[i]
        peak = jnp.maximum(old, score)
        keep = jnp.exp2((old - peak) * SCALE2)
        weight = jnp.exp2((score - peak) * SCALE2)
        return (
            peak,
            lo[i] * keep + weight,
            oo[i] * keep + weight.astype(BF16).astype(F32) * value,
        )

    def new_pair(s):
        own, other = kvown[s].astype(F32), kvpeer[s].astype(F32)
        return jnp.where(is_key, own, other), jnp.where(is_key, other, own)

    h_copy.wait()
    for s in range(1, LONG + 1):
        long_chunk = wrap_y(y - step_l * s)
        short_chunk = wrap_y(y + step_l * s)
        for i in range(4):
            al[s - 1, i].wait_recv()
            forward("long", s, i, long_chunk)
            if s <= SHORT:
                ash[s - 1, i].wait_recv()
                forward("short", s, i, short_chunk)
        if s == 1:
            wait_features(1)
            acc[...] = multiply(1, wf, core, y)
            from_sibling(0, y)
        else:
            from_sibling(s - 1, wrap_y(y + step_l * (s - 1)))
            from_sibling(LONG + s - 1, wrap_y(y - step_l * (s - 1)))
        acc[...] += multiply(1, wf, core, long_chunk)
        if s <= SHORT:
            acc[...] += multiply(1, wf, core, short_chunk)
        if s == 1:
            for copy in p_send:
                copy.wait_recv()
            for i in range(8):
                m2 = rml[:, i:i + 1]
                l2 = rml[:, 8 + i:9 + i]
                m1 = mo[i]
                peak = jnp.maximum(m1, m2)
                e1 = jnp.exp2((m1 - peak) * SCALE2)
                e2 = jnp.exp2((m2 - peak) * SCALE2)
                mo[i] = peak
                lo[i] = lo[i] * e1 + l2 * e2
                oo[i] = oo[i] * e1 + ro[i].astype(F32) * e2
        if s == 2:
            wait_features(0)
            total = jnp.zeros((ROWS, HD), F32)
            for t in range(8):
                total = total + jnp.dot(
                    hf[0, t], wv[t * 1024:(t + 1) * 1024], preferred_element_type=F32)
            e_send = [entry(0, total, bias_ref[...].astype(F32))]
        if s == 3:
            e_send[0].wait_recv()
            key, value = new_pair(0)
            for i in range(8):
                query = qo[i // 4, :, pl.ds(i % 4 * HD, HD)].astype(F32)
                m, l, o = add_entry(0, i, query, key, value)
                if i < 4:
                    out_ref[0, :, pl.ds(i * HD, HD)] = (o / l).astype(BF16)
                else:
                    mo[i], lo[i], oo[i] = m, l, o
            for copy in b_z:
                copy.wait_recv()
    from_sibling(LONG, wrap_y(y + step_l * LONG))

    fresh_bias = bias_row[...].astype(F32)
    for j in range(NZ - 1):
        fresh_bias = fresh_bias + bias_z[j].astype(F32)
    e_send.append(entry(1, acc[...], fresh_bias[:1]))

    for copy in die + [q_send, b_die] + b_y + b_z + p_send + z_send + zg + e_send[:1]:
        copy.wait_send()
    for group_of in (hz, hx, long_send, short_send, al, ash, df):
        for copy in group_of.values():
            copy.wait_send()

    e_send[1].wait_recv()
    key, value = new_pair(1)
    for i in range(4, 8):
        query = qo[1, :, pl.ds((i - 4) * HD, HD)].astype(F32)
        m, l, o = add_entry(1, i, query, key, value)
        out_ref[1, :, pl.ds((i - 4) * HD, HD)] = (o / l).astype(BF16)
    e_send[1].wait_send()


def on_device(hidden, queries, kv_cache, lengths, weights, kv_bias, owner_group):
    sem = pltpu.SemaphoreType.DMA
    vmem = pltpu.VMEM
    any_spec = pl.BlockSpec(memory_space=pl.ANY)
    vmem_spec = pl.BlockSpec(memory_space=pltpu.VMEM)
    scratch = [
        vmem((D, HD), BF16), vmem((HALF, HD), BF16),
        vmem((LONG, CHUNK, HD), BF16), vmem((SHORT, CHUNK, HD), BF16),
        vmem((NZ - 1, QUART, HD), BF16), vmem((D, HD), BF16),
        vmem((2, 8, ROWS, 1024), BF16), vmem((ROWS * 64, 256), BF16),
        vmem((2, ROWS, 512), BF16), vmem((2, ROWS, 512), BF16),
        vmem((8, ROWS, HD), F32), vmem((8, ROWS, HD), F32), vmem((8, ROWS, HD), F32),
        vmem((8, ROWS, HD), BF16), vmem((ROWS, HD), F32),
        vmem((8, ROWS, HD), BF16), vmem((ROWS, HD), F32),
        vmem((ROWS, HD), F32), vmem((2, ROWS, HD), F32), vmem((2, ROWS, HD), F32),
        vmem((16, HD), BF16), vmem((16, HD), BF16), vmem((16, HD), BF16),
        vmem((NY - 1, 16, HD), BF16), vmem((16, HD), BF16), vmem((NZ - 1, 16, HD), BF16),
        vmem((2, ROWS, HD), BF16), vmem((2, ROWS, HD), BF16), vmem((ROWS, HD), F32),
        sem((4,)), sem((NY,)), sem((NY,)),
        sem((LONG, 4)), sem((LONG, 4)), sem((SHORT, 4)), sem((SHORT, 4)),
        sem((3,)), sem((3,)), sem((3,)), sem((3,)),
        sem((LONG, 4)), sem((LONG, 4)), sem((SHORT, 4)), sem((SHORT, 4)),
        sem((NY, 4)), sem((NY, 4)),
        sem((2,)), sem((2,)), sem((2, 2, 3)), sem((2, 2, 3)),
        sem, sem, sem((2,)), sem((2,)), sem((2,)), sem((2,)),
        sem, sem, sem((NY - 1,)), sem((NY - 1,)), sem((NZ - 1,)), sem((NZ - 1,)),
    ]
    return pl.pallas_call(
        kernel,
        out_shape=jax.ShapeDtypeStruct((2, ROWS, 512), BF16),
        in_specs=[any_spec] * 4 + [vmem_spec] * 2 + [pl.BlockSpec(memory_space=pltpu.SMEM)],
        out_specs=vmem_spec,
        scratch_shapes=scratch,
        compiler_params=pltpu.CompilerParams(
            collective_id=0, has_side_effects=True, vmem_limit_bytes=56 << 20),
    )(
        weights.reshape(D, HD), kv_cache.reshape(ROWS * 64, 256), hidden,
        queries.reshape(2, ROWS, 512), lengths.reshape(1, ROWS), kv_bias, owner_group,
    )


def solution(mesh):
    in_specs = (
        P(None, "group", "tp"),
        P(None, "group", "tp", None),
        P("group", "tp", None, None),
        P("group"),
        P("group", None, "tp"),
        P("group", "tp"),
        P(),
    )
    out_specs = P(None, "group", "tp")
    return jax.shard_map(
        on_device, mesh=mesh, in_specs=in_specs, out_specs=out_specs, check_vma=False
    )
```

time: 621 us -> 66.5 us (0.11)
  waiting for transfers between devices: 416 us -> 0 us
  blocking collectives: 145 us -> 0 us
  Pallas kernels: 0 us -> 64.1 us
  starting transfers between devices: 25.2 us -> 0 us
  between operations: 15.9 us -> 0.66 us
  matrix products: 8.51 us -> 0 us
    psum x1 -> x0, waiting for transfers between devices: 411 us -> none  [spread(): return lax.psum(kept, axis)]
    psum x1 -> x0, blocking collectives: 145 us -> none  [spread(): return lax.psum(kept, axis)]
    pallas_call x0 -> x1, Pallas kernels: none -> 64.1 us  [on_device(): pl.pallas_call(kernel, out_shape=jax.ShapeDtypeStruct((2, ROWS, 512), BF1...]
    ppermute x10 -> x0, starting transfers between devices: 25.2 us -> none  [the longest x8 22.6 us: from_partner(): lax.ppermute(x, axis, [(i, i ^ 1 << distance) for i in range(lax.axis_siz...]
    dot_general x9 -> x0, matrix products: 8.51 us -> none  [the longest x2 4.14 us: fold_rows(): jnp.dot(lax.all_gather(panel_rows, 'tp', axis=1, tiled=True), matrix, pre...]
  transfers between devices with their start and end apart: 13 -> 0, of which waited for: 4 -> 0; matrix products, arithmetic and copies ran while one was open for 1% -> 0% of each run, Pallas kernels for 0% -> 0%
where the time goes in v1:
time: 66.5 us; the launch traced here: 66.3 us
  Pallas kernels  64.1 us (96%)
  local copies, waits for them, and re-layouts  1.57 us (2%)
    pallas_call x1, Pallas kernels, on_device(): pl.pallas_call(kernel, out_shape=jax.ShapeDtypeStruct((2, ROWS, 512), BF1...  64.1 us
    unnamed x1, local copies, waits for them, and re-layouts  1.57 us

profile of v1, /device:TPU:1, one launch (start us, length us, event | category | flops | bytes accessed | tf_op | source)
XLA Modules:
  0.0 66.3 jit_solution(8299878967545310070)
XLA Ops:
  0.7 64.1 %shard_map.73 = bf16[2,64,512]{2,1,0:T(8,128)(2,1)} custom-call(bf16[8192,128]{1,0:T(8,128)(2,1)} %bitcast.4, bf16[4096,256]{1,0:T(8,128)(2,1)} %bitcast.5, bf16[2,64,1024]{2,1,0:T(8,128)(2,1)} %hid_hbm.1, bf16[2,64,512]{2,1,0:T(8,128)(2,1)} %bitcast.6, s32[1,64]{1,0:T(1,128)} %bitcast.7, bf16[1,128]{1,0:T(2,128)(2,1)} %bias_ref.1, s32[1]{0:T(128)S(6)} %copy.9.owner_ref), custom_call_target="tpu_custom_call" | custom-call | tf_op jit(solution)/shard_map/pallas_call | solution.py:448
  64.8 1.6 %copy.10 = bf16[2,64,512]{2,1,0:T(8,128)(2,1)} copy(bf16[2,64,512]{2,1,0:T(8,128)(2,1)} %shard_map.73) | data formatting | bytes 262144

commit v2 on v1

v2 whole, which is shorter than its diff:
```python
import math

import jax
import jax.numpy as jnp
from jax import lax
from jax.experimental import pallas as pl
from jax.experimental.pallas import tpu as pltpu
from jax.sharding import PartitionSpec as P

MESH = pl.DeviceIdType.MESH
BF16 = jnp.bfloat16
F32 = jnp.float32
NEG = -1e30
NY, NZ, NX = 8, 4, 4
LONG, SHORT = 4, 3
ROWS, HD, STRIP = 64, 128, 1024
SCALE2 = math.log2(math.e) / math.sqrt(128.0)


def remote(src, dst, send_sem, recv_sem, device):
    return pltpu.make_async_remote_copy(
        src_ref=src, dst_ref=dst, send_sem=send_sem, recv_sem=recv_sem,
        device_id=device, device_id_type=MESH,
    )


def dot_t(a, b):
    return lax.dot_general(a, b, (((1,), (1,)), ((), ())), preferred_element_type=F32)


def kernel(
    w_hbm, kv_hbm, hid_hbm, q_hbm, len_ref, bias_ref, owner_ref, out_ref,
    wv, xbuf, rl, rs, zr, wf, feat, hb, hf, kvv, qo, qp,
    oo, mo, lo, po, pml, ro, rml, lenc, cosf, sinf,
    bias_mine, bias_die, bias_chip, bias_y, bias_row, bias_z,
    part_sib, part_own, part_in, ring_out, ring_in, kvown, kvpeer,
    loc_sem, die_r, rl_r, rs_r, z_r, zg_r, one_s, one_r,
):
    group = lax.axis_index("group")
    tp = lax.axis_index("tp")
    core = group % 2
    y = (group // 2) % NY
    zh = group // (2 * NY)
    x = tp % NX
    zl = tp // NX
    step_l = 1 - 2 * core
    other_core = 1 - core
    lead = core == zl

    def at(zz, yy, cc):
        return (zz * (2 * NY) + yy * 2 + cc, tp)

    def wrap_y(v):
        return (v + 4 * NY) % NY

    sibling = at(zh, y, other_core)
    ahead = at(zh, wrap_y(y + step_l), core)
    behind = at(zh, wrap_y(y - step_l), core)
    z_peers = [at((zh + j) % NZ, y, core) for j in range(1, NZ)]
    y_peers = [at(zh, (y + j) % NY, core) for j in range(1, NY)]
    partner_tp = (tp + NX) % (2 * NX)
    partner = (group, partner_tp)
    x_peers = [(group, zl * NX + (x + j) % NX) for j in range(1, NX)]

    kinds = (
        "die", "long", "short", "z", "zg", "feat_die", "feat_y", "feat_z", "feat_x",
        "hz", "hx", "q", "po", "pml", "bd", "by", "bz", "part", "ring", "e0", "e1",
    )
    slot = {name: i for i, name in enumerate(kinds)}

    def push(kind, src, dst, device, recv_sem=None):
        recv_sem = one_r.at[slot[kind]] if recv_sem is None else recv_sem
        copy = remote(src, dst, one_s.at[slot[kind]], recv_sem, device)
        copy.start()
        return copy

    def take(kind, ref):
        remote(ref, ref, one_s.at[slot[kind]], one_r.at[slot[kind]], sibling).wait_recv()

    def sent(kind, ref):
        remote(ref, ref, one_s.at[slot[kind]], one_r.at[slot[kind]], sibling).wait_send()

    w_copy = pltpu.make_async_copy(w_hbm, wv, loc_sem.at[1])
    q_copy = pltpu.make_async_copy(q_hbm, qo, loc_sem.at[3])
    h_copy = pltpu.make_async_copy(hid_hbm.at[0], hf.at[tp], loc_sem.at[2])
    kv_copy = pltpu.make_async_copy(kv_hbm, kvv, loc_sem.at[0])
    w_copy.start()
    q_copy.start()
    h_copy.start()
    kv_copy.start()

    @pl.when(lead)
    def _():
        pltpu.make_async_copy(hid_hbm.at[1], hb.at[core], loc_sem.at[4]).start()

    barrier = pltpu.get_barrier_semaphore()
    everyone = [sibling, partner] + x_peers + z_peers + y_peers
    for other in everyone:
        pl.semaphore_signal(barrier, inc=1, device_id=other, device_id_type=MESH)
    pl.semaphore_wait(barrier, len(everyone))

    order = []
    for s in range(LONG):
        order.append(wrap_y(y + step_l * (LONG - s)))
        if s < SHORT:
            order.append(wrap_y(y - step_l * (SHORT - s)))
    order.append(y)

    for n in range(NY):
        if n == NY - 1:
            chunk = y
        elif n % 2 == 0:
            chunk = wrap_y(y - step_l * (LONG - n // 2))
        else:
            chunk = wrap_y(y + step_l * (SHORT - n // 2))
        push("die", w_hbm.at[pl.ds(4 * other_core, 4), chunk], xbuf.at[:, chunk], sibling,
             die_r.at[n])

    @pl.when(jnp.logical_not(lead))
    def _():
        push("feat_die", hid_hbm.at[1], hb.at[core], sibling)

    push("q", q_hbm, qp, partner)
    push("hz", hid_hbm.at[0], hf.at[tp], partner)
    for j in range(NX - 1):
        push("hx", hid_hbm.at[0], hf.at[tp], x_peers[j])

    owner = owner_ref[0]
    mine_w = jnp.full((1, HD), (owner == group).astype(F32)).astype(BF16)
    sib_w = jnp.full((1, HD), (owner == group + 1 - 2 * core).astype(F32)).astype(BF16)

    bias_mine[...] = jnp.broadcast_to(bias_ref[...] * mine_w, (16, HD))
    push("bd", bias_mine, bias_die, sibling)

    w_copy.wait()

    def combine(n):
        chunk = order[n]
        remote(xbuf.at[:, chunk], xbuf.at[:, chunk], one_s.at[0], die_r.at[n], sibling).wait_recv()
        for i in range(4):
            xbuf[i, chunk] = wv[4 * core + i, chunk] * mine_w + xbuf[i, chunk] * sib_w

    quarters = [(zh + 1 + n) % NZ for n in range(4)]
    long_send, short_send = {}, {}

    def reduce_step(s):
        chunk = wrap_y(y + step_l * (LONG - s))
        other = wrap_y(y - step_l * (SHORT - s))
        for n in range(4):
            if s == 0:
                src = xbuf.at[quarters[n], chunk]
            else:
                long_send[s - 1, n].wait_recv()
                rl[s - 1, n] = rl[s - 1, n] + xbuf[quarters[n], chunk]
                src = rl.at[s - 1, n]
            long_send[s, n] = push("long", src, rl.at[s, n], ahead, rl_r.at[s, n])
            if s < SHORT:
                if s == 0:
                    src = xbuf.at[quarters[n], other]
                else:
                    short_send[s - 1, n].wait_recv()
                    rs[s - 1, n] = rs[s - 1, n] + xbuf[quarters[n], other]
                    src = rs.at[s - 1, n]
                short_send[s, n] = push("short", src, rs.at[s, n], behind, rs_r.at[s, n])

    combine(0)
    combine(1)
    reduce_step(0)
    for n in range(2, NY):
        combine(n)

    @pl.when(lead)
    def _():
        pltpu.make_async_copy(hid_hbm.at[1], hb.at[core], loc_sem.at[4]).wait()
        take("feat_die", hb.at[other_core])
        pltpu.make_async_copy(
            hb.at[:, :, pl.ds(pl.multiple_of(y * HD, HD), HD)], feat.at[x, y], loc_sem.at[4]
        ).start()
        for j in range(1, NY):
            yy = (y + j) % NY
            push("feat_y", hb.at[:, :, pl.ds(pl.multiple_of(yy * HD, HD), HD)], feat.at[x, y],
                 y_peers[j - 1])

    lens = jnp.broadcast_to(len_ref[...].astype(F32), (ROWS, ROWS))
    diag = lax.broadcasted_iota(jnp.int32, (ROWS, ROWS), 0) == lax.broadcasted_iota(
        jnp.int32, (ROWS, ROWS), 1)
    len_col = jnp.sum(jnp.where(diag, lens, 0.0), axis=1, keepdims=True)
    lenc[...] = jnp.broadcast_to(len_col, (ROWS, HD))

    def attend(block):
        kept = []
        for sub in range(2):
            r0 = block * 16 + sub * 8
            pieces = []
            for src in (qo, qp):
                for s in range(2):
                    for j in range(4):
                        part = src[s, pl.ds(block * 16, 16), pl.ds(j * HD, HD)].astype(F32)
                        pieces.append(part[sub * 8:sub * 8 + 8])
            lhs = jnp.concatenate(pieces, axis=0).astype(BF16)
            cache = pl.ds(r0 * 64, 512)
            scores = dot_t(lhs, kvv[cache, pl.ds(0, HD)]).reshape(16, 8, 512)
            row_id = lax.broadcasted_iota(jnp.int32, (8, 512), 0)
            col_id = lax.broadcasted_iota(jnp.int32, (8, 512), 1)
            length = lenc[pl.ds(r0, 8), :][:, :1]
            pos = (col_id % 64 + zl * 64).astype(F32)
            usable = jnp.logical_and(col_id // 64 == row_id, pos < length)[None]
            peak = jnp.max(jnp.where(usable, scores, NEG), axis=2, keepdims=True)
            weight = jnp.exp2(jnp.where(usable, (scores - peak) * SCALE2, NEG))
            total = jnp.sum(weight, axis=2, keepdims=True)
            weighted = jnp.dot(
                weight.astype(BF16).reshape(128, 512), kvv[cache, pl.ds(HD, HD)],
                preferred_element_type=F32).reshape(16, 8, HD)
            rows = pl.ds(r0, 8)
            oo[:, rows] = weighted[:8]
            mo[:, rows] = jnp.broadcast_to(peak[:8], (8, 8, HD))
            lo[:, rows] = jnp.broadcast_to(total[:8], (8, 8, HD))
            kept.append(weighted[8:])
            lane = lax.broadcasted_iota(jnp.int32, (8, HD), 1)
            packed = jnp.zeros((8, HD), F32)
            for i in range(8):
                packed = jnp.where(lane == i, peak[8 + i], packed)
                packed = jnp.where(lane == 8 + i, total[8 + i], packed)
            pml[rows] = packed
        po[:, pl.ds(block * 16, 16)] = jnp.concatenate(kept, axis=1).astype(BF16)

    q_copy.wait()
    kv_copy.wait()
    take("bd", bias_die)
    bias_chip[...] = bias_mine[...] + bias_die[...]
    for j in range(NY - 1):
        push("by", bias_chip, bias_y.at[j], y_peers[j])
    take("q", qp)
    attend(0)

    reduce_step(1)

    take("hz", hf.at[0])
    for j in range(NX - 1):
        push("hx", hf.at[partner_tp], hf.at[partner_tp], x_peers[j])
    attend(1)

    reduce_step(2)

    def spread_feat():
        for j in range(NX - 1):
            push("feat_x", feat.at[x], feat.at[x], x_peers[j])

    attend(2)

    @pl.when(lead)
    def _():
        pltpu.make_async_copy(
            hb.at[:, :, pl.ds(pl.multiple_of(y * HD, HD), HD)], feat.at[x, y], loc_sem.at[4]
        ).wait()
        take("feat_y", feat.at[0, pl.ds(0, NY - 1)])
        push("feat_z", feat.at[x], feat.at[x], partner)
        spread_feat()

    reduce_step(3)
    attend(3)
    push("po", po, ro, partner)
    push("pml", pml, rml, partner)

    take("by", bias_y)
    total_bias = bias_chip[...]
    for j in range(NY - 1):
        total_bias = total_bias + bias_y[j]
    bias_row[...] = total_bias
    for j in range(NZ - 1):
        push("bz", bias_row, bias_z.at[j], z_peers[j])

    z_send = []
    for n in range(4):
        short_send[SHORT - 1, n].wait_recv()
        long_send[LONG - 1, n].wait_recv()
        rl[LONG - 1, n] = rl[LONG - 1, n] + rs[SHORT - 1, n] + xbuf[quarters[n], y]
        if n < 3:
            z_send.append(push("z", rl.at[LONG - 1, n], zr.at[n], z_peers[n], z_r.at[n]))

    @pl.when(jnp.logical_not(lead))
    def _():
        take("feat_z", feat.at[0])
        spread_feat()

    lane = lax.broadcasted_iota(jnp.int32, (ROWS, HD), 1)
    freq = jnp.exp(-((lane % 64).astype(F32) * (2.0 / HD)) * math.log(1000000.0))
    is_key = tp < NX
    for s in range(2):
        angle = (lenc[...] + float(s)) * freq
        sine = jnp.sin(angle)
        cosf[s] = jnp.where(is_key, jnp.cos(angle), 1.0)
        sinf[s] = jnp.where(is_key, jnp.where(lane < 64, -sine, sine), 0.0)

    total_w = rl[LONG - 1, 3]
    for j in range(NZ - 1):
        z_send[j].wait_recv()
        total_w = total_w + zr[j]
    wf[zh] = total_w
    zg = [push("zg", wf.at[zh], wf.at[zh], z_peers[j], zg_r.at[j]) for j in range(NZ - 1)]

    def entry(s, total, bias):
        total = total + bias
        turned = total * cosf[s] + pltpu.roll(total, 64, 1) * sinf[s]
        kvown[s] = turned.astype(BF16)
        push(f"e{s}", kvown.at[s], kvpeer.at[s], partner)

    h_copy.wait()
    take("hx", hf.at[pl.ds(0, 2 * (NX - 1))])
    total = jnp.zeros((ROWS, HD), F32)
    for t in range(8):
        total = total + jnp.dot(
            hf[t], wv[t].reshape(STRIP, HD), preferred_element_type=F32)
    entry(0, total, bias_ref[...].astype(F32))

    def product(i, cc):
        rows = feat[i, :, cc].reshape(NY * ROWS, HD)
        return jnp.dot(rows, wf[i], preferred_element_type=F32)

    take("feat_x", feat.at[pl.ds(0, NX - 1)])
    part_sib[...] = product(zh, other_core)
    part_own[...] = product(zh, core)
    for j in range(NZ - 1):
        i = (zh - j - 1 + NZ) % NZ
        zg[j].wait_recv()
        part_sib[...] += product(i, other_core)
        if j == NZ - 2:
            push("part", part_sib, part_in, sibling)
        part_own[...] += product(i, core)
    take("part", part_in)
    part_own[...] += part_in[...]
    ring_out[...] = part_own[...].astype(BF16).reshape(NY, ROWS, HD)
    for j in range(1, NY):
        push("ring", ring_out.at[(y + j) % NY], ring_in.at[j - 1], y_peers[j - 1])

    def add_entry(s, i, query, key, value):
        score = jnp.sum(query * key, axis=1, keepdims=True)
        old = mo[i]
        peak = jnp.maximum(old, score)
        keep = jnp.exp2((old - peak) * SCALE2)
        weight = jnp.exp2((score - peak) * SCALE2)
        return (
            peak,
            lo[i] * keep + weight,
            oo[i] * keep + weight.astype(BF16).astype(F32) * value,
        )

    def new_pair(s):
        own, other = kvown[s].astype(F32), kvpeer[s].astype(F32)
        return jnp.where(is_key, own, other), jnp.where(is_key, other, own)

    take("po", ro)
    take("pml", rml)
    take("e0", kvpeer.at[0])
    key, value = new_pair(0)
    for i in range(8):
        m2 = rml[:, i:i + 1]
        l2 = rml[:, 8 + i:9 + i]
        m1 = mo[i]
        peak = jnp.maximum(m1, m2)
        e1 = jnp.exp2((m1 - peak) * SCALE2)
        e2 = jnp.exp2((m2 - peak) * SCALE2)
        mo[i] = peak
        lo[i] = lo[i] * e1 + l2 * e2
        oo[i] = oo[i] * e1 + ro[i].astype(F32) * e2
        query = qo[i // 4, :, pl.ds(i % 4 * HD, HD)].astype(F32)
        m, l, o = add_entry(0, i, query, key, value)
        if i < 4:
            out_ref[0, :, pl.ds(i * HD, HD)] = (o / l).astype(BF16)
        else:
            mo[i], lo[i], oo[i] = m, l, o
    take("bz", bias_z)
    fresh_bias = bias_row[...].astype(F32)
    for j in range(NZ - 1):
        fresh_bias = fresh_bias + bias_z[j].astype(F32)

    sent("die", xbuf)
    sent("long", rl)
    sent("short", rs)
    sent("z", zr)
    sent("zg", zr)
    sent("hz", hf.at[0])
    sent("hx", hf.at[pl.ds(0, 2 * (NX - 1))])
    sent("feat_x", feat.at[pl.ds(0, NX - 1)])
    sent("q", qp)
    sent("po", po)
    sent("pml", pml)
    sent("bd", bias_die)
    sent("by", bias_y)
    sent("bz", bias_z)
    sent("part", part_sib)
    sent("e0", kvown.at[0])

    @pl.when(lead)
    def _():
        sent("feat_y", feat.at[0, pl.ds(0, NY - 1)])
        sent("feat_z", feat.at[0])

    @pl.when(jnp.logical_not(lead))
    def _():
        sent("feat_die", hb.at[0])

    own_rows = pl.ds(pl.multiple_of(y * ROWS, ROWS), ROWS)
    total = part_own[own_rows]
    take("ring", ring_in)
    for j in range(NY - 1):
        total = total + ring_in[j].astype(F32)
    entry(1, total, fresh_bias[:1])
    sent("ring", ring_in)

    take("e1", kvpeer.at[1])
    key, value = new_pair(1)
    for i in range(4, 8):
        query = qo[1, :, pl.ds((i - 4) * HD, HD)].astype(F32)
        m, l, o = add_entry(1, i, query, key, value)
        out_ref[1, :, pl.ds((i - 4) * HD, HD)] = (o / l).astype(BF16)
    sent("e1", kvown.at[1])


def on_device(hidden, queries, kv_cache, lengths, weights, kv_bias, owner_group):
    sem = pltpu.SemaphoreType.DMA
    vmem = pltpu.VMEM
    any_spec = pl.BlockSpec(memory_space=pl.ANY)
    vmem_spec = pl.BlockSpec(memory_space=pltpu.VMEM)
    wide = (8, ROWS, HD)
    scratch = [
        vmem((8, NY, HD, HD), BF16), vmem((4, NY, HD, HD), BF16),
        vmem((LONG, 4, HD, HD), BF16), vmem((SHORT, 4, HD, HD), BF16),
        vmem((NZ - 1, HD, HD), BF16), vmem((4, HD, HD), BF16),
        vmem((NX, NY, 2, ROWS, HD), BF16), vmem((2, ROWS, STRIP), BF16),
        vmem((8, ROWS, STRIP), BF16), vmem((ROWS * 64, 256), BF16),
        vmem((2, ROWS, 512), BF16), vmem((2, ROWS, 512), BF16),
        vmem(wide, F32), vmem(wide, F32), vmem(wide, F32),
        vmem(wide, BF16), vmem((ROWS, HD), F32),
        vmem(wide, BF16), vmem((ROWS, HD), F32),
        vmem((ROWS, HD), F32), vmem((2, ROWS, HD), F32), vmem((2, ROWS, HD), F32),
        vmem((16, HD), BF16), vmem((16, HD), BF16), vmem((16, HD), BF16),
        vmem((NY - 1, 16, HD), BF16), vmem((16, HD), BF16), vmem((NZ - 1, 16, HD), BF16),
        vmem((NY * ROWS, HD), F32), vmem((NY * ROWS, HD), F32), vmem((NY * ROWS, HD), F32),
        vmem(wide, BF16), vmem((NY - 1, ROWS, HD), BF16),
        vmem((2, ROWS, HD), BF16), vmem((2, ROWS, HD), BF16),
        sem((5,)), sem((NY,)), sem((LONG, 4)), sem((SHORT, 4)),
        sem((3,)), sem((3,)), sem((21,)), sem((21,)),
    ]
    return pl.pallas_call(
        kernel,
        out_shape=jax.ShapeDtypeStruct((2, ROWS, 512), BF16),
        in_specs=[any_spec] * 4 + [vmem_spec] * 2 + [pl.BlockSpec(memory_space=pltpu.SMEM)],
        out_specs=vmem_spec,
        scratch_shapes=scratch,
        compiler_params=pltpu.CompilerParams(
            collective_id=0, has_side_effects=True, vmem_limit_bytes=56 << 20),
    )(
        weights.reshape(8, NY, HD, HD), kv_cache.reshape(ROWS * 64, 256), hidden,
        queries.reshape(2, ROWS, 512), lengths.reshape(1, ROWS), kv_bias, owner_group,
    )


def solution(mesh):
    in_specs = (
        P(None, "group", "tp"),
        P(None, "group", "tp", None),
        P("group", "tp", None, None),
        P("group"),
        P("group", None, "tp"),
        P("group", "tp"),
        P(),
    )
    out_specs = P(None, "group", "tp")
    return jax.shard_map(
        on_device, mesh=mesh, in_specs=in_specs, out_specs=out_specs, check_vma=False
    )
```

time: 66.5 us -> 59.7 us (0.90)
  Pallas kernels: 64.1 us -> 57.4 us
    pallas_call x1, Pallas kernels: 64.1 us -> 57.4 us  [on_device(): pl.pallas_call(kernel, out_shape=jax.ShapeDtypeStruct((2, ROWS, 512), BF1...]
where the time goes in v2:
time: 59.7 us; the launch traced here: 59.6 us
  Pallas kernels  57.4 us (96%)
  local copies, waits for them, and re-layouts  1.57 us (3%)
  between operations  0.66 us (1%)
    pallas_call x1, Pallas kernels, on_device(): pl.pallas_call(kernel, out_shape=jax.ShapeDtypeStruct((2, ROWS, 512), BF1...  57.4 us
    unnamed x1, local copies, waits for them, and re-layouts  1.57 us

profile of v2, /device:TPU:1, one launch (start us, length us, event | category | flops | bytes accessed | tf_op | source)
XLA Modules:
  0.0 59.6 jit_solution(2455707415982846618)
XLA Ops:
  0.7 57.4 %shard_map.73 = bf16[2,64,512]{2,1,0:T(8,128)(2,1)} custom-call(bf16[8,8,128,128]{3,2,1,0:T(8,128)(2,1)} %bitcast.4, bf16[4096,256]{1,0:T(8,128)(2,1)} %bitcast.5, bf16[2,64,1024]{2,1,0:T(8,128)(2,1)} %hid_hbm.1, bf16[2,64,512]{2,1,0:T(8,128)(2,1)} %bitcast.6, s32[1,64]{1,0:T(1,128)} %bitcast.7, bf16[1,128]{1,0:T(2,128)(2,1)} %bias_ref.1, s32[1]{0:T(128)S(6)} %copy.9.owner_ref), custom_call_target="tpu_custom_call" | custom-call | tf_op jit(solution)/shard_map/pallas_call | solution.py:445
  58.0 1.6 %copy.10 = bf16[2,64,512]{2,1,0:T(8,128)(2,1)} copy(bf16[2,64,512]{2,1,0:T(8,128)(2,1)} %shard_map.73) | data formatting | bytes 262144

commit v3 on v2

--- a/solution.py
+++ b/solution.py
@@ -29,8 +29,9 @@
 
 
 def kernel(
-    w_hbm, kv_hbm, hid_hbm, q_hbm, len_ref, bias_ref, owner_ref, out_ref,
-    wv, xbuf, rl, rs, zr, wf, feat, hb, hf, kvv, qo, qp,
+    w_hbm, kv_hbm, hid_hbm, q_hbm, len_hbm, bias_hbm, owner_hbm, out_ref,
+    len_ref, bias_ref, owner_ref,
+    wv, xbuf, rl, rs, zr, wf, feat, hf, kvv, qo, qp,
     oo, mo, lo, po, pml, ro, rml, lenc, cosf, sinf,
     bias_mine, bias_die, bias_chip, bias_y, bias_row, bias_z,
     part_sib, part_own, part_in, ring_out, ring_in, kvown, kvpeer,
@@ -89,12 +90,24 @@
     h_copy.start()
     kv_copy.start()
 
+    small = [
+        pltpu.make_async_copy(len_hbm, len_ref, loc_sem.at[5]),
+        pltpu.make_async_copy(bias_hbm, bias_ref, loc_sem.at[6]),
+        pltpu.make_async_copy(owner_hbm, owner_ref, loc_sem.at[7]),
+    ]
+    for copy in small:
+        copy.start()
+
+    def strip(yy):
+        return hid_hbm.at[1, :, pl.ds(pl.multiple_of(yy * HD, HD), HD)]
+
     @pl.when(lead)
     def _():
-        pltpu.make_async_copy(hid_hbm.at[1], hb.at[core], loc_sem.at[4]).start()
+        pltpu.make_async_copy(strip(y), feat.at[x, y, core], loc_sem.at[4]).start()
 
     barrier = pltpu.get_barrier_semaphore()
-    everyone = [sibling, partner] + x_peers + z_peers + y_peers
+    cross = [at(zh, (y + j) % NY, other_core) for j in range(1, NY)]
+    everyone = [sibling, partner] + x_peers + z_peers + y_peers + cross
     for other in everyone:
         pl.semaphore_signal(barrier, inc=1, device_id=other, device_id_type=MESH)
     pl.semaphore_wait(barrier, len(everyone))
@@ -115,16 +128,22 @@
             chunk = wrap_y(y + step_l * (SHORT - n // 2))
         push("die", w_hbm.at[pl.ds(4 * other_core, 4), chunk], xbuf.at[:, chunk], sibling,
              die_r.at[n])
+        if n == 1:
+            for j in range(1, NY):
+                yy = (y + j) % NY
+                push("feat_y", strip(yy), feat.at[x, y, core], at(zh, yy, zl))
 
     @pl.when(jnp.logical_not(lead))
     def _():
-        push("feat_die", hid_hbm.at[1], hb.at[core], sibling)
+        push("feat_die", strip(y), feat.at[x, y, core], sibling)
 
     push("q", q_hbm, qp, partner)
     push("hz", hid_hbm.at[0], hf.at[tp], partner)
     for j in range(NX - 1):
         push("hx", hid_hbm.at[0], hf.at[tp], x_peers[j])
 
+    for copy in small:
+        copy.wait()
     owner = owner_ref[0]
     mine_w = jnp.full((1, HD), (owner == group).astype(F32)).astype(BF16)
     sib_w = jnp.full((1, HD), (owner == group + 1 - 2 * core).astype(F32)).astype(BF16)
@@ -168,18 +187,6 @@
     reduce_step(0)
     for n in range(2, NY):
         combine(n)
-
-    @pl.when(lead)
-    def _():
-        pltpu.make_async_copy(hid_hbm.at[1], hb.at[core], loc_sem.at[4]).wait()
-        take("feat_die", hb.at[other_core])
-        pltpu.make_async_copy(
-            hb.at[:, :, pl.ds(pl.multiple_of(y * HD, HD), HD)], feat.at[x, y], loc_sem.at[4]
-        ).start()
-        for j in range(1, NY):
-            yy = (y + j) % NY
-            push("feat_y", hb.at[:, :, pl.ds(pl.multiple_of(yy * HD, HD), HD)], feat.at[x, y],
-                 y_peers[j - 1])
 
     lens = jnp.broadcast_to(len_ref[...].astype(F32), (ROWS, ROWS))
     diag = lax.broadcasted_iota(jnp.int32, (ROWS, ROWS), 0) == lax.broadcasted_iota(
@@ -235,29 +242,33 @@
 
     reduce_step(1)
 
+    def spread_feat():
+        for j in range(NX - 1):
+            push("feat_x", feat.at[x], feat.at[x], x_peers[j])
+
+    @pl.when(lead)
+    def _():
+        pltpu.make_async_copy(strip(y), feat.at[x, y, core], loc_sem.at[4]).wait()
+        take("feat_y", feat.at[0, pl.ds(0, NY - 1)])
+        take("feat_die", feat.at[0, 0, 0])
+        push("feat_z", feat.at[x], feat.at[x], partner)
+        spread_feat()
+
     take("hz", hf.at[0])
     for j in range(NX - 1):
         push("hx", hf.at[partner_tp], hf.at[partner_tp], x_peers[j])
     attend(1)
 
     reduce_step(2)
-
-    def spread_feat():
-        for j in range(NX - 1):
-            push("feat_x", feat.at[x], feat.at[x], x_peers[j])
-
     attend(2)
 
-    @pl.when(lead)
-    def _():
-        pltpu.make_async_copy(
-            hb.at[:, :, pl.ds(pl.multiple_of(y * HD, HD), HD)], feat.at[x, y], loc_sem.at[4]
-        ).wait()
-        take("feat_y", feat.at[0, pl.ds(0, NY - 1)])
-        push("feat_z", feat.at[x], feat.at[x], partner)
+    reduce_step(3)
+
+    @pl.when(jnp.logical_not(lead))
+    def _():
+        take("feat_z", feat.at[0])
         spread_feat()
 
-    reduce_step(3)
     attend(3)
     push("po", po, ro, partner)
     push("pml", pml, rml, partner)
@@ -277,11 +288,6 @@
         rl[LONG - 1, n] = rl[LONG - 1, n] + rs[SHORT - 1, n] + xbuf[quarters[n], y]
         if n < 3:
             z_send.append(push("z", rl.at[LONG - 1, n], zr.at[n], z_peers[n], z_r.at[n]))
-
-    @pl.when(jnp.logical_not(lead))
-    def _():
-        take("feat_z", feat.at[0])
-        spread_feat()
 
     lane = lax.broadcasted_iota(jnp.int32, (ROWS, HD), 1)
     freq = jnp.exp(-((lane % 64).astype(F32) * (2.0 / HD)) * math.log(1000000.0))
@@ -390,15 +396,15 @@
     sent("bz", bias_z)
     sent("part", part_sib)
     sent("e0", kvown.at[0])
+    sent("feat_y", ring_in)
 
     @pl.when(lead)
     def _():
-        sent("feat_y", feat.at[0, pl.ds(0, NY - 1)])
         sent("feat_z", feat.at[0])
 
     @pl.when(jnp.logical_not(lead))
     def _():
-        sent("feat_die", hb.at[0])
+        sent("feat_die", kvown.at[0])
 
     own_rows = pl.ds(pl.multiple_of(y * ROWS, ROWS), ROWS)
     total = part_own[own_rows]
@@ -424,10 +430,11 @@
     vmem_spec = pl.BlockSpec(memory_space=pltpu.VMEM)
     wide = (8, ROWS, HD)
     scratch = [
+        vmem((1, ROWS), jnp.int32), vmem((1, HD), BF16), pltpu.SMEM((1,), jnp.int32),
         vmem((8, NY, HD, HD), BF16), vmem((4, NY, HD, HD), BF16),
         vmem((LONG, 4, HD, HD), BF16), vmem((SHORT, 4, HD, HD), BF16),
         vmem((NZ - 1, HD, HD), BF16), vmem((4, HD, HD), BF16),
-        vmem((NX, NY, 2, ROWS, HD), BF16), vmem((2, ROWS, STRIP), BF16),
+        vmem((NX, NY, 2, ROWS, HD), BF16),
         vmem((8, ROWS, STRIP), BF16), vmem((ROWS * 64, 256), BF16),
         vmem((2, ROWS, 512), BF16), vmem((2, ROWS, 512), BF16),
         vmem(wide, F32), vmem(wide, F32), vmem(wide, F32),
@@ -439,20 +446,21 @@
         vmem((NY * ROWS, HD), F32), vmem((NY * ROWS, HD), F32), vmem((NY * ROWS, HD), F32),
         vmem(wide, BF16), vmem((NY - 1, ROWS, HD), BF16),
         vmem((2, ROWS, HD), BF16), vmem((2, ROWS, HD), BF16),
-        sem((5,)), sem((NY,)), sem((LONG, 4)), sem((SHORT, 4)),
+        sem((8,)), sem((NY,)), sem((LONG, 4)), sem((SHORT, 4)),
         sem((3,)), sem((3,)), sem((21,)), sem((21,)),
     ]
     return pl.pallas_call(
         kernel,
         out_shape=jax.ShapeDtypeStruct((2, ROWS, 512), BF16),
-        in_specs=[any_spec] * 4 + [vmem_spec] * 2 + [pl.BlockSpec(memory_space=pltpu.SMEM)],
+        in_specs=[any_spec] * 7,
         out_specs=vmem_spec,
         scratch_shapes=scratch,
         compiler_params=pltpu.CompilerParams(
             collective_id=0, has_side_effects=True, vmem_limit_bytes=56 << 20),
     )(
         weights.reshape(8, NY, HD, HD), kv_cache.reshape(ROWS * 64, 256), hidden,
-        queries.reshape(2, ROWS, 512), lengths.reshape(1, ROWS), kv_bias, owner_group,
+        queries.reshape(2, ROWS, 512), lengths.reshape(1, ROWS), kv_bias,
+        owner_group,
     )
 
 

time: 59.7 us -> 56.5 us (0.946)
  Pallas kernels: 57.4 us -> 54.1 us
    pallas_call x1, Pallas kernels: 57.4 us -> 54.1 us  [on_device(): pl.pallas_call(kernel, out_shape=jax.ShapeDtypeStruct((2, ROWS, 512), BF1...]
where the time goes in v3:
time: 56.5 us; the launch traced here: 56.3 us
  Pallas kernels  54.1 us (96%)
  local copies, waits for them, and re-layouts  1.57 us (3%)
  between operations  0.66 us (1%)
    pallas_call x1, Pallas kernels, on_device(): pl.pallas_call(kernel, out_shape=jax.ShapeDtypeStruct((2, ROWS, 512), BF1...  54.1 us
    unnamed x1, local copies, waits for them, and re-layouts  1.57 us

profile of v3, /device:TPU:1, one launch (start us, length us, event | category | flops | bytes accessed | tf_op | source)
XLA Modules:
  0.0 56.3 jit_solution(9038620790418592175)
XLA Ops:
  0.7 54.1 %shard_map.73 = bf16[2,64,512]{2,1,0:T(8,128)(2,1)} custom-call(bf16[8,8,128,128]{3,2,1,0:T(8,128)(2,1)} %bitcast.4, bf16[4096,256]{1,0:T(8,128)(2,1)} %bitcast.5, bf16[2,64,1024]{2,1,0:T(8,128)(2,1)} %hid_hbm.1, bf16[2,64,512]{2,1,0:T(8,128)(2,1)} %bitcast.6, s32[1,64]{1,0:T(1,128)} %bitcast.7, bf16[1,128]{1,0:T(2,128)(2,1)} %bias_hbm.1, s32[1]{0:T(128)S(6)} %copy.9.owner_hbm), custom_call_target="tpu_custom_call" | custom-call | tf_op jit(solution)/shard_map/pallas_call | solution.py:452
  54.8 1.6 %copy.10 = bf16[2,64,512]{2,1,0:T(8,128)(2,1)} copy(bf16[2,64,512]{2,1,0:T(8,128)(2,1)} %shard_map.73) | data formatting | bytes 262144

commit v4 on v3

--- a/solution.py
+++ b/solution.py
@@ -451,7 +451,7 @@
     ]
     return pl.pallas_call(
         kernel,
-        out_shape=jax.ShapeDtypeStruct((2, ROWS, 512), BF16),
+        out_shape=pltpu.VMEM((2, ROWS, 512), BF16),
         in_specs=[any_spec] * 7,
         out_specs=vmem_spec,
         scratch_shapes=scratch,

time: 56.5 us -> 54.9 us (0.972)
  local copies, waits for them, and re-layouts: 1.57 us -> 0.66 us
  Pallas kernels: 54.1 us -> 53.5 us
    unnamed x1, local copies, waits for them, and re-layouts: 1.57 us -> 0.66 us
    pallas_call x1, Pallas kernels: 54.1 us -> 53.5 us  [on_device(): pl.pallas_call(kernel, out_shape=pltpu.VMEM((2, ROWS, 512), BF16), in_spe...]
where the time goes in v4:
time: 54.9 us; the launch traced here: 54.8 us
  Pallas kernels  53.5 us (97%)
  local copies, waits for them, and re-layouts  0.66 us (1%)
  between operations  0.66 us (1%)
    pallas_call x1, Pallas kernels, on_device(): pl.pallas_call(kernel, out_shape=pltpu.VMEM((2, ROWS, 512), BF16), in_spe...  53.5 us

profile of v4, /device:TPU:1, one launch (start us, length us, event | category | flops | bytes accessed | tf_op | source)
XLA Modules:
  0.0 54.8 jit_solution(17684227145258725777)
XLA Ops:
  0.7 53.5 %shard_map.73 = bf16[2,64,512]{2,1,0:T(8,128)(2,1)S(1)} custom-call(bf16[8,8,128,128]{3,2,1,0:T(8,128)(2,1)} %bitcast.4, bf16[4096,256]{1,0:T(8,128)(2,1)} %bitcast.5, bf16[2,64,1024]{2,1,0:T(8,128)(2,1)} %hid_hbm.1, bf16[2,64,512]{2,1,0:T(8,128)(2,1)} %bitcast.6, s32[1,64]{1,0:T(1,128)} %bitcast.7, bf16[1,128]{1,0:T(2,128)(2,1)} %bias_hbm.1, ...), custom_call_target="tpu_custom_call" | custom-call | tf_op jit(solution)/shard_map/pallas_call | solution.py:452
  54.1 0.7 %copy.9 = bf16[2,64,512]{2,1,0:T(8,128)(2,1)} copy(bf16[2,64,512]{2,1,0:T(8,128)(2,1)S(1)} %shard_map.73) | data formatting | bytes 262144

commit v5 on v4

--- a/solution.py
+++ b/solution.py
@@ -235,8 +235,6 @@
     kv_copy.wait()
     take("bd", bias_die)
     bias_chip[...] = bias_mine[...] + bias_die[...]
-    for j in range(NY - 1):
-        push("by", bias_chip, bias_y.at[j], y_peers[j])
     take("q", qp)
     attend(0)
 
@@ -272,14 +270,6 @@
     attend(3)
     push("po", po, ro, partner)
     push("pml", pml, rml, partner)
-
-    take("by", bias_y)
-    total_bias = bias_chip[...]
-    for j in range(NY - 1):
-        total_bias = total_bias + bias_y[j]
-    bias_row[...] = total_bias
-    for j in range(NZ - 1):
-        push("bz", bias_row, bias_z.at[j], z_peers[j])
 
     z_send = []
     for n in range(4):
@@ -288,6 +278,9 @@
         rl[LONG - 1, n] = rl[LONG - 1, n] + rs[SHORT - 1, n] + xbuf[quarters[n], y]
         if n < 3:
             z_send.append(push("z", rl.at[LONG - 1, n], zr.at[n], z_peers[n], z_r.at[n]))
+
+    for j in range(NY - 1):
+        push("by", bias_chip, bias_y.at[j], y_peers[j])
 
     lane = lax.broadcasted_iota(jnp.int32, (ROWS, HD), 1)
     freq = jnp.exp(-((lane % 64).astype(F32) * (2.0 / HD)) * math.log(1000000.0))
@@ -305,19 +298,19 @@
     wf[zh] = total_w
     zg = [push("zg", wf.at[zh], wf.at[zh], z_peers[j], zg_r.at[j]) for j in range(NZ - 1)]
 
+    take("by", bias_y)
+    total_bias = bias_chip[...]
+    for j in range(NY - 1):
+        total_bias = total_bias + bias_y[j]
+    bias_row[...] = total_bias
+    for j in range(NZ - 1):
+        push("bz", bias_row, bias_z.at[j], z_peers[j])
+
     def entry(s, total, bias):
         total = total + bias
         turned = total * cosf[s] + pltpu.roll(total, 64, 1) * sinf[s]
         kvown[s] = turned.astype(BF16)
         push(f"e{s}", kvown.at[s], kvpeer.at[s], partner)
-
-    h_copy.wait()
-    take("hx", hf.at[pl.ds(0, 2 * (NX - 1))])
-    total = jnp.zeros((ROWS, HD), F32)
-    for t in range(8):
-        total = total + jnp.dot(
-            hf[t], wv[t].reshape(STRIP, HD), preferred_element_type=F32)
-    entry(0, total, bias_ref[...].astype(F32))
 
     def product(i, cc):
         rows = feat[i, :, cc].reshape(NY * ROWS, HD)
@@ -338,6 +331,14 @@
     ring_out[...] = part_own[...].astype(BF16).reshape(NY, ROWS, HD)
     for j in range(1, NY):
         push("ring", ring_out.at[(y + j) % NY], ring_in.at[j - 1], y_peers[j - 1])
+
+    h_copy.wait()
+    take("hx", hf.at[pl.ds(0, 2 * (NX - 1))])
+    total = jnp.zeros((ROWS, HD), F32)
+    for t in range(8):
+        total = total + jnp.dot(
+            hf[t], wv[t].reshape(STRIP, HD), preferred_element_type=F32)
+    entry(0, total, bias_ref[...].astype(F32))
 
     def add_entry(s, i, query, key, value):
         score = jnp.sum(query * key, axis=1, keepdims=True)

time: 54.9 us -> 54.5 us (level)
  no operation moved by 1% of the time
where the time goes in v5:
time: 54.5 us; the launch traced here: 54.4 us
  Pallas kernels  53 us (97%)
  local copies, waits for them, and re-layouts  0.66 us (1%)
  between operations  0.66 us (1%)
    pallas_call x1, Pallas kernels, on_device(): pl.pallas_call(kernel, out_shape=pltpu.VMEM((2, ROWS, 512), BF16), in_spe...  53 us

profile of v5, /device:TPU:1, one launch (start us, length us, event | category | flops | bytes accessed | tf_op | source)
XLA Modules:
  0.0 54.4 jit_solution(10323189883133917478)
XLA Ops:
  0.7 53.0 %shard_map.73 = bf16[2,64,512]{2,1,0:T(8,128)(2,1)S(1)} custom-call(bf16[8,8,128,128]{3,2,1,0:T(8,128)(2,1)} %bitcast.4, bf16[4096,256]{1,0:T(8,128)(2,1)} %bitcast.5, bf16[2,64,1024]{2,1,0:T(8,128)(2,1)} %hid_hbm.1, bf16[2,64,512]{2,1,0:T(8,128)(2,1)} %bitcast.6, s32[1,64]{1,0:T(1,128)} %bitcast.7, bf16[1,128]{1,0:T(2,128)(2,1)} %bias_hbm.1, ...), custom_call_target="tpu_custom_call" | custom-call | tf_op jit(solution)/shard_map/pallas_call | solution.py:453
  53.7 0.7 %copy.9 = bf16[2,64,512]{2,1,0:T(8,128)(2,1)} copy(bf16[2,64,512]{2,1,0:T(8,128)(2,1)S(1)} %shard_map.73) | data formatting | bytes 262144
